TPU v7x, 32 devices: a whole 2x2x4 slice. The times are simulated.
32 devices in a mesh: ctx: 16 (over z, y, core), tp: 2 (over x).
Axes of the slice: x: 2, y: 2, z: 4, core: 2. Of those that a mesh axis runs over, the one named last changes fastest.
Arguments:
- queries: bfloat16 [4096, 4096], P('ctx', 'tp'), may hold values from -5 to 5
- key_head_array: bfloat16 [4096, 1024], P('ctx', 'tp'), may hold values from -8 to 8
- value_head_array: bfloat16 [4096, 1024], P('ctx', 'tp'), may hold values from -6 to 6
- ssm_input: bfloat16 [4096, 4096], P('ctx', 'tp'), may hold values from -6 to 6
- ssm_gate: bfloat16 [4096, 4096], P('ctx', 'tp'), may hold values from -30 to 30
- ssm_write: bfloat16 [4096, 1024], P('ctx', 'tp'), may hold values from -2.5 to 2.5
- ssm_read: bfloat16 [4096, 1024], P('ctx', 'tp'), may hold values from -2.5 to 2.5
- step_size: float32 [64, 4096], P('tp', 'ctx'), may hold values from 0.005 to 0.1
- log_decay: float32 [64, 4096], P('tp', 'ctx'), may hold values from -1 to 0
- skip_gain: float32 [64], P('tp'), may hold values from 0.5 to 2
- norm_gain: float32 [4096], P('tp'), may hold values from 0.1 to 1.9
- out_weight: bfloat16 [4096, 2048], P('tp'), may hold values from -2 to 2
Outputs:
- attn_mixed: float32 [4096, 2048], P('ctx', 'tp')
- ssm_output: float32 [4096, 4096], P('ctx', 'tp')
All inputs are finite; a program needn't handle non-finite values.
Results may differ from a plain program's by a relative error of at most 0.0053.
Values may be sent and summed in bfloat16 or wider, within the bound.
No kernel may reach another device: no remote copies, remote signals or barrier semaphores. Data moves between devices by JAX's collectives and lax.ppermute only.
A program may use at most 128 MiB of HBM per device.

v0:
```python
import math
import jax
import jax.numpy as jnp
from jax import lax
from jax.sharding import PartitionSpec as P

HEAD_SIZE = 128
P_SIZE = 64
NS = 128
neg_big = -1e30


def prefix_2(x, axis, combine, identity, reverse):
    count, mine = (lax.axis_size(axis), lax.axis_index(axis))
    everything = jax.tree.map(lambda part: lax.all_gather(part, axis), x)
    start = jax.tree.map(
        lambda part, zero: jnp.broadcast_to(jnp.asarray(zero, part.dtype), part.shape), x, identity
    )

    def lap(k, before):
        at = count - 1 - k if reverse else k
        reached = at > mine if reverse else at < mine
        new = combine(before, jax.tree.map(lambda part: part[at], everything))
        return jax.tree.map(lambda a, b: jnp.where(reached, a, b), new, before)

    return lax.fori_loop(0, count, lap, start)


def broadcast(x, axis, root):
    mine = lax.axis_index(axis) == root
    return lax.psum(jnp.where(mine, x, jnp.zeros_like(x)), axis)


def online_update(running, query_blk, key_blk, value_blk, query_pos, key_pos, score_scale):
    top_old, total_old, acc_old = running
    scores = (
        jnp.einsum("qgrd,kgd->grqk", query_blk, key_blk, preferred_element_type=jnp.float32)
        * score_scale
    )
    allowed = key_pos[None, None, None, :] <= query_pos[None, None, :, None]
    top_block = jnp.max(jnp.where(allowed, scores, neg_big), axis=-1)
    top_new = jnp.maximum(top_old, top_block)
    weights = jnp.where(allowed, jnp.exp(scores - top_new[..., None]), 0.0)
    factor = jnp.exp(top_old - top_new)
    total_new = total_old * factor + jnp.sum(weights, axis=-1)
    acc_new = acc_old * factor[..., None] + jnp.einsum(
        "grqk,kgd->grqd",
        weights.astype(jnp.bfloat16),
        value_blk,
        preferred_element_type=jnp.float32,
    )
    return (top_new, total_new, acc_new)


def compose(earlier, later):
    return (earlier[0] * later[0], later[0][..., None, None] * earlier[1] + later[1])


def steps_for():
    return 4


def body(
    queries,
    key_head_array,
    value_head_array,
    ssm_input,
    ssm_gate,
    ssm_write,
    ssm_read,
    step_size,
    log_decay,
    skip_gain,
    norm_gain,
    out_weight,
):
    ctx_count = lax.axis_size("ctx")
    ctx_index = lax.axis_index("ctx")
    tok_dev = queries.shape[0]
    half = tok_dev // 2
    kv_dev = key_head_array.shape[1] // HEAD_SIZE
    heads_dev = queries.shape[1] // HEAD_SIZE
    group_repeat = heads_dev // kv_dev
    score_scale = 1.0 / math.sqrt(HEAD_SIZE)
    last_block = 2 * ctx_count - 1
    row_ids = jnp.arange(half, dtype=jnp.int32)
    early_qpos = ctx_index * half + row_ids
    late_qpos = (last_block - ctx_index) * half + row_ids
    query_early = queries[:half].reshape(half, kv_dev, group_repeat, HEAD_SIZE)
    query_late = queries[half:].reshape(half, kv_dev, group_repeat, HEAD_SIZE)

    def fresh_state():
        return (
            jnp.full((kv_dev, group_repeat, half), neg_big, jnp.float32),
            jnp.zeros((kv_dev, group_repeat, half), jnp.float32),
            jnp.zeros((kv_dev, group_repeat, half, HEAD_SIZE), jnp.float32),
        )

    key_piece = lax.all_gather(key_head_array, "ctx", axis=0, tiled=True)
    value_piece = lax.all_gather(value_head_array, "ctx", axis=0, tiled=True)
    shard_count = key_piece.shape[0] // tok_dev
    per_step = steps_for()
    turns = shard_count // per_step
    key_groups = key_piece.reshape(turns, per_step, 2, half, kv_dev, HEAD_SIZE)
    value_groups = value_piece.reshape(turns, per_step, 2, half, kv_dev, HEAD_SIZE)

    def one_turn(running_pair, inputs):
        key_grp, value_grp, turn_index = inputs
        base_shard = turn_index * per_step
        shard_ids = base_shard + jnp.arange(per_step, dtype=jnp.int32)
        early_kpos = (shard_ids[:, None] * half + row_ids[None, :]).reshape(-1)
        late_kpos = ((last_block - shard_ids)[:, None] * half + row_ids[None, :]).reshape(-1)
        early_keys = key_grp[:, 0].reshape(per_step * half, kv_dev, HEAD_SIZE)
        late_keys = key_grp[:, 1].reshape(per_step * half, kv_dev, HEAD_SIZE)
        early_vals = value_grp[:, 0].reshape(per_step * half, kv_dev, HEAD_SIZE)
        late_vals = value_grp[:, 1].reshape(per_step * half, kv_dev, HEAD_SIZE)
        run_early, run_late = running_pair
        run_early = lax.cond(
            base_shard <= ctx_index,
            lambda running_now: online_update(
                running_now,
                query_early,
                early_keys,
                early_vals,
                early_qpos,
                early_kpos,
                score_scale,
            ),
            lambda running_now: running_now,
            run_early,
        )
        run_late = online_update(
            run_late, query_late, early_keys, early_vals, late_qpos, early_kpos, score_scale
        )
        run_late = lax.cond(
            base_shard + per_step - 1 >= ctx_index,
            lambda running_now: online_update(
                running_now, query_late, late_keys, late_vals, late_qpos, late_kpos, score_scale
            ),
            lambda running_now: running_now,
            run_late,
        )
        return ((run_early, run_late), None)

    result_pair, unused_out = lax.scan(
        one_turn,
        (fresh_state(), fresh_state()),
        (key_groups, value_groups, jnp.arange(turns, dtype=jnp.int32)),
    )

    def finish(running):
        top_fin, total_fin, acc_fin = running
        heads_out = acc_fin / total_fin[..., None]
        return (
            jnp.transpose(heads_out, (2, 0, 1, 3))
            .reshape(half, heads_dev * HEAD_SIZE)
            .astype(jnp.bfloat16)
        )

    attn_heads = jnp.concatenate([finish(result_pair[0]), finish(result_pair[1])], axis=0)
    head_terms = jnp.dot(attn_heads, out_weight, preferred_element_type=jnp.float32)
    attn_mixed = lax.psum_scatter(head_terms, "tp", scatter_dimension=1, tiled=True)
    heads_ssm = step_size.shape[0]
    groups_dev = ssm_write.shape[1] // NS
    per_group = heads_ssm // groups_dev
    causal = row_ids[:, None] >= row_ids[None, :]
    skip_cols = skip_gain.reshape(groups_dev, per_group)
    gain_cols = norm_gain.reshape(groups_dev, per_group * P_SIZE)

    def block_parts(row_from):
        cum_decay = jnp.cumsum(log_decay[:, row_from : row_from + half], axis=1).reshape(
            groups_dev, per_group, half
        )
        step_blk = step_size[:, row_from : row_from + half].reshape(groups_dev, per_group, half)
        input_blk = ssm_input[row_from : row_from + half].reshape(
            half, groups_dev, per_group, P_SIZE
        )
        write_blk = ssm_write[row_from : row_from + half].reshape(half, groups_dev, NS)
        read_blk = ssm_read[row_from : row_from + half].reshape(half, groups_dev, NS)
        scaled = (
            input_blk.astype(jnp.float32) * jnp.transpose(step_blk, (2, 0, 1))[..., None]
        ).astype(jnp.bfloat16)
        inner_prod = jnp.einsum(
            "tgn,sgn->gts", read_blk, write_blk, preferred_element_type=jnp.float32
        )
        decay_gap = cum_decay[..., :, None] - cum_decay[..., None, :]
        mixing = jnp.where(
            causal, inner_prod[:, None] * jnp.exp(jnp.where(causal, decay_gap, 0.0)), 0.0
        ).astype(jnp.bfloat16)
        local_out = jnp.einsum(
            "gjts,sgjp->tgjp", mixing, scaled, preferred_element_type=jnp.float32
        )
        tail_decay = jnp.exp(cum_decay[..., -1:] - cum_decay)
        written = (
            jnp.transpose(write_blk, (1, 0, 2)).astype(jnp.float32)[:, None] * tail_decay[..., None]
        ).astype(jnp.bfloat16)
        block_state = jnp.einsum(
            "sgjp,gjsn->gjpn", scaled, written, preferred_element_type=jnp.float32
        )
        block_decay = jnp.exp(cum_decay[..., -1])
        return ((block_decay, block_state), (local_out, cum_decay, read_blk, input_blk, row_from))

    def block_output(entering, pieces):
        local_out, cum_decay, read_blk, input_blk, row_from = pieces
        carried = jnp.einsum(
            "tgn,gjpn->tgjp",
            read_blk.astype(jnp.float32),
            entering,
            precision=lax.Precision.HIGHEST,
        )
        mixed_out = (
            local_out
            + carried * jnp.transpose(jnp.exp(cum_decay), (2, 0, 1))[..., None]
            + skip_cols[None, :, :, None] * input_blk.astype(jnp.float32)
        )
        gate_blk = ssm_gate[row_from : row_from + half].reshape(
            half, groups_dev, per_group * P_SIZE
        )
        gated = mixed_out.reshape(half, groups_dev, per_group * P_SIZE) * jax.nn.silu(
            gate_blk.astype(jnp.float32)
        )
        mean_square = jnp.mean(gated * gated, axis=-1, keepdims=True)
        normed = gated * lax.rsqrt(mean_square + 1e-05) * gain_cols[None]
        return normed.reshape(half, heads_ssm * P_SIZE)

    early_elem, early_rest = block_parts(0)
    late_elem, late_rest = block_parts(half)
    unit_decay = jnp.ones((groups_dev, per_group), jnp.float32)
    zero_state = jnp.zeros((groups_dev, per_group, P_SIZE, NS), jnp.float32)
    prefix = prefix_2(
        (early_elem[0], early_elem[1]), "ctx", compose, (unit_decay, zero_state), False
    )
    inclusive = compose(prefix, early_elem)
    total_state = broadcast(inclusive[1], "ctx", ctx_count - 1)
    suffix = prefix_2((late_elem[0], late_elem[1]), "ctx", compose, (unit_decay, zero_state), True)
    late_entering = suffix[0][..., None, None] * total_state + suffix[1]
    ssm_output = jnp.concatenate(
        [block_output(prefix[1], early_rest), block_output(late_entering, late_rest)], axis=0
    )
    return (attn_mixed, ssm_output)


def solution(mesh):
    placed = (
        P("ctx", "tp"),
        P("ctx", "tp"),
        P("ctx", "tp"),
        P("ctx", "tp"),
        P("ctx", "tp"),
        P("ctx", "tp"),
        P("ctx", "tp"),
        P("tp", "ctx"),
        P("tp", "ctx"),
        P("tp"),
        P("tp"),
        P("tp", None),
    )
    return jax.shard_map(
        body,
        mesh=mesh,
        in_specs=placed,
        out_specs=(P("ctx", "tp"), P("ctx", "tp")),
        check_vma=False,
    )
```

profile of v0, /device:TPU:0, one launch (start us, length us, event | category | flops | bytes accessed | tf_op | source)
XLA Modules:
  0.0 505.0 jit_solution(12839579409607009505)
XLA Ops:
  19.7 2.2 reduce_window_sum.24
  24.7 2.5 fusion.67
  36.9 2.2 fusion.92
  42.0 24.4 %all-gather = f32[64,8,1]{1,2,0:T(1,128)} all-gather(f32[4,8,1]{1,2,0:T(1,128)} %bitcast.327), channel_id=2, replica_groups=mesh['ctx'=16,'tp'=2] {'ctx'}, dimensions={0}, use_global_device_ids=true | all-gather | bytes 2176 | tf_op jit(solution)/shard_map/all_gather | solution.py:15
  66.4 19.0 %all-gather.2 = f32[64,8,1]{1,2,0:T(1,128)} all-gather(f32[4,8,1]{1,2,0:T(1,128)} %bitcast.328), channel_id=4, replica_groups=mesh['ctx'=16,'tp'=2] {'ctx'}, dimensions={0}, use_global_device_ids=true | all-gather | bytes 2176 | tf_op jit(solution)/shard_map/all_gather | solution.py:15
  87.9 2.7 convolution_bitcast_fusion.2
  90.7 1.9 convolution_bitcast_fusion.3
  92.6 7.0 %reshape.295 = bf16[4,4,2,128,4,128]{5,4,3,2,1,0:T(4,128)(2,1)} reshape(bf16[4096,512]{1,0:T(8,128)(2,1)} %all-gather.9.cloned.1.call-done) | data formatting | bytes 8388608 | tf_op jit(solution)/shard_map/reshape | solution.py:104
  99.5 15.5 %all-gather.11.cloned.1.call-done = bf16[4096,512]{1,0:T(8,128)(2,1)} async-done(((bf16[256,512]{1,0:T(8,128)(2,1)}), bf16[4096,512]{1,0:T(8,128)(2,1)}) %all-gather.11.cloned.1.call-update) | async-done | bytes 4194320 | tf_op jit(solution)/shard_map/all_gather | solution.py:100
  115.0 6.9 %reshape.296 = bf16[4,4,2,128,4,128]{5,4,3,2,1,0:T(4,128)(2,1)} reshape(bf16[4096,512]{1,0:T(8,128)(2,1)} %all-gather.11.cloned.1.call-done) | data formatting | bytes 8388608 | tf_op jit(solution)/shard_map/reshape | solution.py:105
  124.1 57.9 %while.58 = (s32[]{:T(128)}, f32[4,4,128]{2,1,0:T(4,128)S(1)}, f32[4,4,128]{2,1,0:T(4,128)S(1)}, f32[4,4,128,128]{3,2,1,0:T(8,128)}, f32[4,4,128]{2,1,0:T(4,128)...) while((s32[]{:T(128)}, f32[4,4,128]{2,1,0:T(4,128)S(1)}, ...), condition=%wide.region_11.12_spmd.clone.clone, body=%wide.region_0.11_spmd.clone.clone.sunk | while | flops 1646999296 | bytes 91899224 | solution.py:145
  125.7 2.3 constant_dynamic-slice_fusion.3
  132.8 4.5 conditional.9
  137.3 5.6 %conditional.8 = ((f32[4,4,128]{2,1,0:T(4,128)S(1)}, f32[4,4,128]{2,1,0:T(4,128)S(1)}, f32[4,4,128,128]{3,2,1,0:T(8,128)})) conditional(s32[]{:T(128)} %convert_element_type.198, (f32[4,4,128]{2,1,0:T(4,128)S(1)}, f32[4,4,128]{2,1,0:T(4,128)S(1)}, f32[4,4,128,128]{3,2,1,0:T(8,128)}) %tuple.174, (s32[4]{0:T(128)S(1)}, s32[128]{0:T(128)S(1)}, ...), branch_computations={%region_1.1_spmd, %region_2.4_spmd} | conditional | flops 548999808 | bytes 27138184 | solution.py:118
  144.3 2.3 constant_dynamic-slice_fusion.3
  151.4 4.5 conditional.9
  157.3 2.3 constant_dynamic-slice_fusion.3
  164.4 4.5 conditional.9
  170.4 2.3 constant_dynamic-slice_fusion.3
  177.4 4.5 conditional.9
  186.4 56.2 %all-gather.13.cloned.1.call-done = f32[64,8,64,128]{3,2,1,0:T(8,128)} async-done(((f32[4,8,64,128]{3,2,1,0:T(8,128)}), f32[64,8,64,128]{3,2,1,0:T(8,128)}) %all-gather.13.cloned.1.call-update) | async-done | bytes 16777232 | tf_op jit(solution)/shard_map/all_gather | solution.py:15
  242.6 34.7 %while.59 = (s32[]{:T(128)}, f32[4,8,64,128]{3,2,1,0:T(8,128)S(1)}, s32[]{:T(128)}, f32[16,4,8]{2,1,0:T(4,128)}, f32[16,4,8,64,128]{4,3,2,1,0:T(8,128)}, /*index=5*/s32[]{:T(128)}, s32[]{:T(128)}) while((s32[]{:T(128)}, f32[4,8,64,128]{3,2,1,0:T(8,128)S(1)}, s32[]{:T(128)}, f32[16,4,8]{2,1,0:T(4,128)}, ...), condition=%wide.region_15.16_spmd.clone, body=%wide.region_14.15_spmd.clone.sunk | while | flops 1048580 | bytes 3146217 | solution.py:26
  278.7 7.2 %fusion.68 = f32[256,2048]{1,0:T(8,128)} fusion(bf16[2048,2048]{1,0:T(8,128)(2,1)} %param.33, bf16[128,2048]{0,1:T(8,128)(2,1)S(1)} %bitcast.292, bf16[128,2048]{0,1:T(8,128)(2,1)S(1)} %bitcast.293), kind=kOutput, calls=%fused_computation.96 | convolution fusion | flops 2149580800 | bytes 11534336 | tf_op jit(solution)/shard_map/dot_general | solution.py:161
  285.9 83.8 %all-gather.15.cloned.1.call-done = f32[64,8,64,128]{3,2,1,0:T(8,128)} async-done(((f32[4,8,64,128]{3,2,1,0:T(8,128)}), f32[64,8,64,128]{3,2,1,0:T(8,128)}) %all-gather.15.cloned.1.call-update) | async-done | bytes 16777232 | tf_op jit(solution)/shard_map/all_gather | solution.py:15
  369.7 34.7 %while.60 = (s32[]{:T(128)}, f32[4,8]{1,0:T(4,128)S(1)}, f32[4,8,64,128]{3,2,1,0:T(8,128)S(1)}, s32[]{:T(128)}, f32[16,4,8]{2,1,0:T(4,128)}, /*index=5*/f32[16,4...) while((s32[]{:T(128)}, f32[4,8]{1,0:T(4,128)S(1)}, ...), condition=%wide.region_19.20_spmd.clone, body=%wide.region_18.19_spmd.clone.sunk | while | flops 1048680 | bytes 3146545 | solution.py:26
  404.5 3.5 multiply_reduce_fusion.1
  408.7 2.5 copy.128
  411.2 53.2 %all-reduce.2.cloned.1.call-done = f32[4,8,64,128]{3,2,1,0:T(8,128)} async-done(((f32[4,8,64,128]{3,2,1,0:T(8,128)}), f32[4,8,64,128]{3,2,1,0:T(8,128)}) %all-reduce.2.cloned.1.call-update) | async-done | bytes 1048592 | tf_op jit(solution)/shard_map/psum | solution.py:31
  464.4 3.9 multiply_reduce_fusion
  470.0 2.5 copy.140
  472.6 2.4 multiply_multiply_fusion.1
  476.5 21.7 %reduce-scatter.2.cloned.1.call-done = f32[256,1024]{1,0:T(8,128)} async-done(((f32[256,2048]{1,0:T(8,128)}), f32[256,1024]{1,0:T(8,128)}) %reduce-scatter.2.cloned.1.call-update) | async-done | bytes 1048592 | tf_op jit(solution)/shard_map/reduce_scatter | solution.py:162
  (355 shorter events, 155.9 us)
Async XLA Ops:
  7.2 85.4 %all-gather.9.cloned.1.call-start = ((), (), s32[]{:S(2)}) async-start(), calls=%async_computation.1 | async-start | bytes 4456448 | tf_op jit(solution)/shard_map/all_gather | solution.py:99
  7.9 107.1 %all-gather.11.cloned.1.call-start = ((), (), s32[]{:S(2)}) async-start(), calls=%async_computation.2 | async-start | bytes 4456448 | tf_op jit(solution)/shard_map/all_gather | solution.py:100
  8.6 233.9 %all-gather.13.cloned.1.call-start = ((), (), s32[]{:S(2)}) async-start(), calls=%async_computation.5 | async-start | bytes 17825792 | tf_op jit(solution)/shard_map/all_gather | solution.py:15
  13.6 77.0 %copy-start.5 = (f32[128,2048]{0,1:T(8,128)}, f32[128,2048]{0,1:T(8,128)S(1)}, u32[]{:S(2)}) copy-start(f32[128,2048]{0,1:T(8,128)S(1)} %copy.119) | copy-start | bytes 3145732
  16.6 6.4 %copy-start.23 = (f32[128,4,8]{0,2,1:T(8,128)}, f32[128,4,8]{0,2,1:T(8,128)S(1)}, u32[]{:S(2)}) copy-start(f32[128,4,8]{0,2,1:T(8,128)S(1)} %get-tuple-element.990) | copy-start | bytes 49156
  19.6 350.1 %all-gather.15.cloned.1.call-start = ((), (), s32[]{:S(2)}) async-start(), calls=%async_computation.6 | async-start | bytes 17825792 | tf_op jit(solution)/shard_map/all_gather | solution.py:15
  23.0 6.7 %copy-start.7 = (f32[128,2048]{0,1:T(8,128)}, f32[128,2048]{0,1:T(8,128)S(1)}, u32[]{:S(2)}) copy-start(f32[128,2048]{0,1:T(8,128)S(1)} %copy.131) | copy-start | bytes 3145732
  23.0 5.5 %copy-start.26 = (f32[4,8,1]{1,0,2:T(4,128)S(1)}, f32[4,8,1]{1,0,2:T(4,128)}, u32[]{:S(2)}) copy-start(f32[4,8,1]{1,0,2:T(4,128)} %copy.171) | copy-start | bytes 388
  23.0 6.0 %copy-start.21 = (bf16[256,512]{1,0:T(8,128)(2,1)S(1)}, bf16[256,512]{1,0:T(8,128)(2,1)}, u32[]{:S(2)}) copy-start(bf16[256,512]{1,0:T(8,128)(2,1)} %param.28) | copy-start | bytes 786436
  27.3 437.2 %all-reduce.2.cloned.1.call-start = ((), (), s32[]{:S(2)}) async-start(), calls=%async_computation.4 | async-start | bytes 2097152 | tf_op jit(solution)/shard_map/psum | solution.py:31
  36.9 51.0 %copy-start.8 = (f32[128,2048]{0,1:T(8,128)S(1)}, f32[128,2048]{0,1:T(8,128)}, u32[]{:S(2)}) copy-start(f32[128,2048]{0,1:T(8,128)} %copy-done.7) | copy-start | bytes 3145732
  42.0 48.7 %copy-start.24 = (f32[128,4,8]{0,2,1:T(8,128)S(1)}, f32[128,4,8]{0,2,1:T(8,128)}, u32[]{:S(2)}) copy-start(f32[128,4,8]{0,2,1:T(8,128)} %copy-done.23) | copy-start | bytes 49156
  133.1 1.7 copy-start.15
  137.5 2.8 copy-start.3
  137.5 2.8 copy-start.11
  151.7 1.7 copy-start.15
  177.7 1.7 copy-start.15
  181.9 60.7 %copy-start = (f32[4,8,64,128]{3,2,1,0:T(8,128)S(1)}, f32[4,8,64,128]{3,2,1,0:T(8,128)}, u32[]{:S(2)}) copy-start(f32[4,8,64,128]{3,2,1,0:T(8,128)} %custom-call) | copy-start | bytes 3145732
  242.6 34.7 %copy-start.4 = (f32[4,8,64,128]{3,2,1,0:T(8,128)S(1)}, f32[4,8,64,128]{3,2,1,0:T(8,128)}, u32[]{:S(2)}) copy-start(f32[4,8,64,128]{3,2,1,0:T(8,128)} %fusion.66) | copy-start | bytes 3145732
  242.6 34.7 %copy-start.29 = (f32[4,8]{1,0:T(4,128)S(1)}, f32[4,8]{1,0:T(4,128)}, u32[]{:S(2)}) copy-start(f32[4,8]{1,0:T(4,128)} %bitcast_exponential_fusion) | copy-start | bytes 388
  278.5 219.7 %reduce-scatter.2.cloned.1.call-start = ((), (), s32[]{:S(2)}) async-start(), calls=%async_computation.3 | async-start | bytes 3145728 | tf_op jit(solution)/shard_map/reduce_scatter | solution.py:162
  278.7 91.0 %copy-start.1 = (f32[4,8,64,128]{3,2,1,0:T(8,128)S(1)}, f32[4,8,64,128]{3,2,1,0:T(8,128)}, u32[]{:S(2)}) copy-start(f32[4,8,64,128]{3,2,1,0:T(8,128)} %custom-call.2) | copy-start | bytes 3145732
  278.7 91.0 %copy-start.25 = (f32[4,8]{1,0:T(4,128)S(1)}, f32[4,8]{1,0:T(4,128)}, u32[]{:S(2)}) copy-start(f32[4,8]{1,0:T(4,128)} %custom-call.1) | copy-start | bytes 388
  369.7 34.8 %copy-start.6 = (f32[128,2048]{0,1:T(8,128)S(1)}, f32[128,2048]{0,1:T(8,128)}, u32[]{:S(2)}) copy-start(f32[128,2048]{0,1:T(8,128)} %copy-done.5) | copy-start | bytes 3145732
  369.7 34.8 %copy-start.20 = (bf16[128,512]{0,1:T(8,128)(2,1)S(1)}, bf16[128,512]{0,1:T(8,128)(2,1)}, u32[]{:S(2)}) copy-start(bf16[128,512]{0,1:T(8,128)(2,1)} %copy.166) | copy-start | bytes 393220
  369.7 34.8 %copy-start.27 = (f32[128,4,8]{0,2,1:T(8,128)S(1)}, f32[128,4,8]{0,2,1:T(8,128)}, u32[]{:S(2)}) copy-start(f32[128,4,8]{0,2,1:T(8,128)} %get-tuple-element.994) | copy-start | bytes 49156
  369.7 34.8 %copy-start.31 = (f32[4,8]{1,0:T(4,128)S(1)}, f32[4,8]{1,0:T(4,128)}, u32[]{:S(2)}) copy-start(f32[4,8]{1,0:T(4,128)} %mul.374) | copy-start | bytes 388
  408.0 56.5 %copy-start.9 = (f32[128,2048]{0,1:T(8,128)S(1)}, f32[128,2048]{0,1:T(8,128)}, u32[]{:S(2)}) copy-start(f32[128,2048]{0,1:T(8,128)} %copy-done.7) | copy-start | bytes 3145732
  408.0 56.5 %copy-start.28 = (f32[128,4,8]{0,2,1:T(8,128)S(1)}, f32[128,4,8]{0,2,1:T(8,128)}, u32[]{:S(2)}) copy-start(f32[128,4,8]{0,2,1:T(8,128)} %get-tuple-element.996) | copy-start | bytes 49156
  468.3 4.2 copy-start.10
  468.3 4.2 copy-start.17
  468.3 4.2 copy-start.30
  (21 other events, 25.3 us)
Sparse Core Ops, SparseCore 0:
  10.2 53.4 all-gather.8
  65.8 49.1 all-gather.10
  117.2 125.3 all-gather.12
  244.6 125.0 all-gather.14
  373.0 91.3 all-reduce.1
  467.1 31.0 reduce-scatter.1
where the time goes:
time: 509 us; the launch traced here: 505 us
  waiting for transfers between devices  232 us (46%)
  other arithmetic  82.9 us (16%)
  local copies, waits for them, and re-layouts  81.4 us (16%)
  matrix products  46.4 us (9%)
  blocking collectives  43.4 us (9%)
  between operations  14.5 us (3%)
    all_gather x2, waiting for transfers between devices, prefix_2(): everything = jax.tree.map(lambda part: lax.all_gather(part, axis), x)  140 us
    select_n x48, other arithmetic, lap(): return jax.tree.map(lambda a, b: jnp.where(reached, a, b), new, before)  57.9 us
    psum x1, waiting for transfers between devices, broadcast(): return lax.psum(jnp.where(mine, x, jnp.zeros_like(x)), axis)  53.2 us
    all_gather x2, blocking collectives, prefix_2(): everything = jax.tree.map(lambda part: lax.all_gather(part, axis), x)  43.4 us
    reduce_scatter x1, waiting for transfers between devices, body(): lax.psum_scatter(head_terms, 'tp', scatter_dimension=1, tiled=True)  21.7 us
    all_gather x1, waiting for transfers between devices, body(): value_piece = lax.all_gather(value_head_array, 'ctx', axis=0, tiled=True)  15.5 us
    dot_general x9, matrix products, online_update(): jnp.einsum('grqk,kgd->grqd', weights.astype(jnp.bfloat16), value_blk, pre...  13.6 us
    dynamic_slice x16, local copies, waits for them, and re-layouts, body(): lax.scan(one_turn, (fresh_state(), fresh_state()), (key_groups, value_gro...  13.4 us
  transfers between devices with their start and end apart: 6, of which 5 were waited for; matrix products, arithmetic and copies ran while one was open for 40% of the time, Pallas kernels for 0%

commit v1 on v0

--- a/solution.py
+++ b/solution.py
@@ -97,7 +97,18 @@
         )
 
     key_piece = lax.all_gather(key_head_array, "ctx", axis=0, tiled=True)
-    value_piece = lax.all_gather(value_head_array, "ctx", axis=0, tiled=True)
+    ways = lax.axis_size("ctx")
+    up = [(d, (d + 1) % ways) for d in range(ways)]
+    down = [(d, (d - 1) % ways) for d in range(ways)]
+    earlier_2, later_2 = ([value_head_array], [value_head_array])
+    for _ in range(ways // 2):
+        earlier_2.append(lax.ppermute(earlier_2[-1], "ctx", up))
+    for _ in range((ways - 1) // 2):
+        later_2.append(lax.ppermute(later_2[-1], "ctx", down))
+    line = jnp.concatenate([*earlier_2[::-1], *later_2[1:]], axis=0)
+    value_piece = jnp.roll(
+        line, (lax.axis_index("ctx") - ways // 2) * value_head_array.shape[0], axis=0
+    )
     shard_count = key_piece.shape[0] // tok_dev
     per_step = steps_for()
     turns = shard_count // per_step

time: 509 us -> 484 us (0.951)
  waiting for transfers between devices: 232 us -> 164 us
  starting transfers between devices: 0.24 us -> 29 us
  local copies, waits for them, and re-layouts: 81.4 us -> 97.1 us
    all_gather x2, waiting for transfers between devices: 140 us -> 47.5 us  [prefix_2(): everything = jax.tree.map(lambda part: lax.all_gather(part, axis), x)]
    ppermute x0 -> x15, waiting for transfers between devices: none -> 41.2 us  [the longest x8 21.5 us: body(): earlier_2.append(lax.ppermute(earlier_2[-1], 'ctx', up))]
    ppermute x0 -> x15, starting transfers between devices: none -> 28.8 us  [the longest x7 28.2 us: body(): later_2.append(lax.ppermute(later_2[-1], 'ctx', down))]
    all_gather x1 -> x0, waiting for transfers between devices: 15.5 us -> none  [body(): value_piece = lax.all_gather(value_head_array, 'ctx', axis=0, tiled=True)]
    unnamed x60 -> x129, local copies, waits for them, and re-layouts: 8.05 us -> 21 us
  transfers between devices with their start and end apart: 6 -> 20, of which waited for: 5 -> 13; matrix products, arithmetic and copies ran while one was open for 40% -> 46% of each run, Pallas kernels for 0% -> 0%
where the time goes in v1:
time: 484 us; the launch traced here: 480 us
  waiting for transfers between devices  164 us (34%)
  local copies, waits for them, and re-layouts  97.1 us (20%)
  other arithmetic  83.2 us (17%)
  matrix products  47.6 us (10%)
  blocking collectives  39.9 us (8%)
  starting transfers between devices  29 us (6%)
  between operations  14.5 us (3%)
    select_n x48, other arithmetic, lap(): return jax.tree.map(lambda a, b: jnp.where(reached, a, b), new, before)  58.1 us
    psum x1, waiting for transfers between devices, broadcast(): return lax.psum(jnp.where(mine, x, jnp.zeros_like(x)), axis)  53.2 us
    all_gather x2, waiting for transfers between devices, prefix_2(): everything = jax.tree.map(lambda part: lax.all_gather(part, axis), x)  47.5 us
    all_gather x2, blocking collectives, prefix_2(): everything = jax.tree.map(lambda part: lax.all_gather(part, axis), x)  39.9 us
    ppermute x7, starting transfers between devices, body(): later_2.append(lax.ppermute(later_2[-1], 'ctx', down))  28.2 us
    reduce_scatter x1, waiting for transfers between devices, body(): lax.psum_scatter(head_terms, 'tp', scatter_dimension=1, tiled=True)  21.7 us
    ppermute x8, waiting for transfers between devices, body(): earlier_2.append(lax.ppermute(earlier_2[-1], 'ctx', up))  21.5 us
    unnamed x129, local copies, waits for them, and re-layouts  21 us
  transfers between devices with their start and end apart: 20, of which 13 were waited for; matrix products, arithmetic and copies ran while one was open for 46% of the time, Pallas kernels for 0%

profile of v1, /device:TPU:0, one launch (start us, length us, event | category | flops | bytes accessed | tf_op | source)
XLA Modules:
  0.0 479.8 jit_solution(8197840397143316918)
XLA Ops:
  25.6 12.1 %collective-permute-done = bf16[256,512]{1,0:T(8,128)(2,1)S(1)} collective-permute-done((bf16[256,512]{1,0:T(8,128)(2,1)S(1)}, bf16[256,512]{1,0:T(8,128)(2,1)S(1)}, u32[]{:S(2)}, u32[]{:S(2)}) %collective-permute-start) | collective-permute-done | bytes 262176 | tf_op jit(solution)/shard_map/ppermute | solution.py:105
  37.8 4.4 collective-permute-start.8
  42.2 6.2 %collective-permute-done.1 = bf16[256,512]{1,0:T(8,128)(2,1)S(1)} collective-permute-done((bf16[256,512]{1,0:T(8,128)(2,1)S(1)}, bf16[256,512]{1,0:T(8,128)(2,1)S(1)}, u32[]{:S(2)}, u32[]{:S(2)}) %collective-permute-start.1) | collective-permute-done | bytes 262176 | tf_op jit(solution)/shard_map/ppermute | solution.py:105
  51.1 4.6 collective-permute-start.9
  61.6 4.4 collective-permute-start.10
  71.4 4.7 collective-permute-start.11
  87.8 20.1 %all-gather = f32[64,8,1]{1,2,0:T(1,128)} all-gather(f32[4,8,1]{1,2,0:T(1,128)S(1)} %bitcast.327), channel_id=2, replica_groups=mesh['ctx'=16,'tp'=2] {'ctx'}, dimensions={0}, use_global_device_ids=true | all-gather | bytes 2176 | tf_op jit(solution)/shard_map/all_gather | solution.py:15
  108.0 19.7 %all-gather.2 = f32[64,8,1]{1,2,0:T(1,128)} all-gather(f32[4,8,1]{1,2,0:T(1,128)S(1)} %bitcast.328), channel_id=4, replica_groups=mesh['ctx'=16,'tp'=2] {'ctx'}, dimensions={0}, use_global_device_ids=true | all-gather | bytes 2176 | tf_op jit(solution)/shard_map/all_gather | solution.py:15
  128.9 3.5 convolution_bitcast_fusion.2
  132.4 6.2 %collective-permute-done.12 = bf16[256,512]{1,0:T(8,128)(2,1)S(1)} collective-permute-done((bf16[256,512]{1,0:T(8,128)(2,1)}, bf16[256,512]{1,0:T(8,128)(2,1)S(1)}, u32[]{:S(2)}, u32[]{:S(2)}) %collective-permute-start.12) | collective-permute-done | bytes 262176 | tf_op jit(solution)/shard_map/ppermute | solution.py:107
  138.6 4.5 collective-permute-start.13
  143.1 2.7 convolution_bitcast_fusion.3
  145.8 6.8 %collective-permute-done.13 = bf16[256,512]{1,0:T(8,128)(2,1)S(1)} collective-permute-done((bf16[256,512]{1,0:T(8,128)(2,1)S(1)}, bf16[256,512]{1,0:T(8,128)(2,1)S(1)}, u32[]{:S(2)}, u32[]{:S(2)}) %collective-permute-start.13) | collective-permute-done | bytes 262176 | tf_op jit(solution)/shard_map/ppermute | solution.py:107
  152.6 4.6 collective-permute-start.14
  163.4 3.3 collective-permute-done.14
  175.2 7.0 %reshape.296 = bf16[4,4,2,128,4,128]{5,4,3,2,1,0:T(4,128)(2,1)} reshape(bf16[4096,512]{1,0:T(8,128)(2,1)} %constant_dynamic-slice_fusion.2) | data formatting | bytes 8388608 | tf_op jit(solution)/shard_map/reshape | solution.py:116
  182.2 6.9 %reshape.295 = bf16[4,4,2,128,4,128]{5,4,3,2,1,0:T(4,128)(2,1)} reshape(bf16[4096,512]{1,0:T(8,128)(2,1)} %all-gather.8.cloned.1.call-done) | data formatting | bytes 8388608 | tf_op jit(solution)/shard_map/reshape | solution.py:115
  191.3 57.9 %while.58 = (s32[]{:T(128)}, f32[4,4,128]{2,1,0:T(4,128)S(1)}, f32[4,4,128]{2,1,0:T(4,128)S(1)}, f32[4,4,128,128]{3,2,1,0:T(8,128)}, f32[4,4,128]{2,1,0:T(4,128)...) while((s32[]{:T(128)}, f32[4,4,128]{2,1,0:T(4,128)S(1)}, ...), condition=%wide.region_11.12_spmd.clone.clone, body=%wide.region_0.11_spmd.clone.clone.sunk | while | flops 1646999296 | bytes 91899224 | solution.py:156
  199.8 4.5 conditional.9
  204.3 5.6 %conditional.8 = ((f32[4,4,128]{2,1,0:T(4,128)S(1)}, f32[4,4,128]{2,1,0:T(4,128)S(1)}, f32[4,4,128,128]{3,2,1,0:T(8,128)})) conditional(s32[]{:T(128)} %convert_element_type.198, (f32[4,4,128]{2,1,0:T(4,128)S(1)}, f32[4,4,128]{2,1,0:T(4,128)S(1)}, f32[4,4,128,128]{3,2,1,0:T(8,128)}) %tuple.174, (s32[4]{0:T(128)S(1)}, s32[128]{0:T(128)S(1)}, ...), branch_computations={%region_1.1_spmd, %region_2.4_spmd} | conditional | flops 548999808 | bytes 27138184 | solution.py:129
  218.4 4.5 conditional.9
  231.7 4.5 conditional.9
  244.7 4.5 conditional.9
  253.7 34.9 %while.59 = (s32[]{:T(128)}, f32[4,8,64,128]{3,2,1,0:T(8,128)S(1)}, s32[]{:T(128)}, f32[16,4,8]{2,1,0:T(4,128)}, f32[16,4,8,64,128]{4,3,2,1,0:T(8,128)}, /*index=5*/s32[]{:T(128)}, s32[]{:T(128)}) while((s32[]{:T(128)}, f32[4,8,64,128]{3,2,1,0:T(8,128)S(1)}, s32[]{:T(128)}, f32[16,4,8]{2,1,0:T(4,128)}, ...), condition=%wide.region_15.16_spmd.clone, body=%wide.region_14.15_spmd.clone.sunk | while | flops 1048580 | bytes 3146217 | solution.py:26
  290.0 7.1 %fusion.68 = f32[256,2048]{1,0:T(8,128)} fusion(bf16[2048,2048]{1,0:T(8,128)(2,1)} %param.33, bf16[128,2048]{0,1:T(8,128)(2,1)S(1)} %bitcast.292, bf16[128,2048]{0,1:T(8,128)(2,1)S(1)} %bitcast.293), kind=kOutput, calls=%fused_computation.96 | convolution fusion | flops 2149580800 | bytes 11534336 | tf_op jit(solution)/shard_map/dot_general | solution.py:172
  297.1 47.5 %all-gather.12.cloned.1.call-done = f32[64,8,64,128]{3,2,1,0:T(8,128)} async-done(((f32[4,8,64,128]{3,2,1,0:T(8,128)}), f32[64,8,64,128]{3,2,1,0:T(8,128)}) %all-gather.12.cloned.1.call-update) | async-done | bytes 16777232 | tf_op jit(solution)/shard_map/all_gather | solution.py:15
  344.7 34.9 %while.60 = (s32[]{:T(128)}, f32[4,8]{1,0:T(4,128)S(1)}, f32[4,8,64,128]{3,2,1,0:T(8,128)S(1)}, s32[]{:T(128)}, f32[16,4,8]{2,1,0:T(4,128)}, /*index=5*/f32[16,4...) while((s32[]{:T(128)}, f32[4,8]{1,0:T(4,128)S(1)}, ...), condition=%wide.region_19.20_spmd.clone, body=%wide.region_18.19_spmd.clone.sunk | while | flops 1048680 | bytes 3146545 | solution.py:26
  379.7 3.5 multiply_reduce_fusion.1
  383.8 2.6 copy.128
  386.4 53.2 %all-reduce.2.cloned.1.call-done = f32[4,8,64,128]{3,2,1,0:T(8,128)} async-done(((f32[4,8,64,128]{3,2,1,0:T(8,128)}), f32[4,8,64,128]{3,2,1,0:T(8,128)}) %all-reduce.2.cloned.1.call-update) | async-done | bytes 1048592 | tf_op jit(solution)/shard_map/psum | solution.py:31
  439.5 3.9 multiply_reduce_fusion
  451.6 21.7 %reduce-scatter.2.cloned.1.call-done = f32[256,1024]{1,0:T(8,128)} async-done(((f32[256,2048]{1,0:T(8,128)}), f32[256,1024]{1,0:T(8,128)}) %reduce-scatter.2.cloned.1.call-update) | async-done | bytes 1048592 | tf_op jit(solution)/shard_map/reduce_scatter | solution.py:173
  (453 shorter events, 199.9 us)
Async XLA Ops:
  7.2 175.0 %all-gather.8.cloned.1.call-start = ((), (), s32[]{:S(2)}) async-start(), calls=%async_computation.1 | async-start | bytes 4456448 | tf_op jit(solution)/shard_map/all_gather | solution.py:99
  7.9 245.7 %all-gather.10.cloned.1.call-start = ((), (), s32[]{:S(2)}) async-start(), calls=%async_computation.4 | async-start | bytes 17825792 | tf_op jit(solution)/shard_map/all_gather | solution.py:15
  16.5 328.2 %all-gather.12.cloned.1.call-start = ((), (), s32[]{:S(2)}) async-start(), calls=%async_computation.5 | async-start | bytes 17825792 | tf_op jit(solution)/shard_map/all_gather | solution.py:15
  22.5 44.0 %copy-start.41 = (f32[4,8,1]{1,0,2:T(4,128)S(1)}, f32[4,8,1]{1,0,2:T(4,128)}, u32[]{:S(2)}) copy-start(f32[4,8,1]{1,0,2:T(4,128)} %copy-done.40) | copy-start | bytes 388
  25.1 414.4 %all-reduce.2.cloned.1.call-start = ((), (), s32[]{:S(2)}) async-start(), calls=%async_computation.3 | async-start | bytes 2097152 | tf_op jit(solution)/shard_map/psum | solution.py:31
  25.1 12.6 %collective-permute-start = (bf16[256,512]{1,0:T(8,128)(2,1)S(1)}, bf16[256,512]{1,0:T(8,128)(2,1)S(1)}, u32[]{:S(2)}, u32[]{:S(2)}) collective-permute-start(bf16[256,512]{1,0:T(8,128)(2,1)S(1)} %copy-done.20), channel_id=1, source_target_pairs={{0,2},{2,4},{4,6},{6,8},{8,10},{10,12},{12,14},{14,16},{16,18},{18... | collective-permute-start | bytes 786440 | tf_op jit(solution)/shard_map/ppermute | solution.py:105
  37.8 10.7 %collective-permute-start.1 = (bf16[256,512]{1,0:T(8,128)(2,1)S(1)}, bf16[256,512]{1,0:T(8,128)(2,1)S(1)}, u32[]{:S(2)}, u32[]{:S(2)}) collective-permute-start(bf16[256,512]{1,0:T(8,128)(2,1)S(1)} %collective-permute-done), channel_id=1, source_target_pairs={{0,2},{2,4},{4,6},{6,8},{8,10},{10,12},{12,14},{14,16},{16,18},{18... | collective-permute-start | bytes 786440 | tf_op jit(solution)/shard_map/ppermute | solution.py:105
  37.8 13.3 %collective-permute-start.8 = (bf16[256,512]{1,0:T(8,128)(2,1)S(1)}, bf16[256,512]{1,0:T(8,128)(2,1)S(1)}, u32[]{:S(2)}, u32[]{:S(2)}) collective-permute-start(bf16[256,512]{1,0:T(8,128)(2,1)S(1)} %copy-done.20), channel_id=1, source_target_pairs={{0,30},{2,0},{4,2},{6,4},{8,6},{10,8},{12,10},{14,12},{16,14},{18,... | collective-permute-start | bytes 786440 | tf_op jit(solution)/shard_map/ppermute | solution.py:107
  48.4 9.3 %collective-permute-start.2 = (bf16[256,512]{1,0:T(8,128)(2,1)S(1)}, bf16[256,512]{1,0:T(8,128)(2,1)S(1)}, u32[]{:S(2)}, u32[]{:S(2)}) collective-permute-start(bf16[256,512]{1,0:T(8,128)(2,1)S(1)} %collective-permute-done.1), channel_id=1, source_target_pairs={{0,2},{2,4},{4,6},{6,8},{8,10},{10,12},{12,14},{14,16},{16,18},{18... | collective-permute-start | bytes 786440 | tf_op jit(solution)/shard_map/ppermute | solution.py:105
  51.1 10.6 %collective-permute-start.9 = (bf16[256,512]{1,0:T(8,128)(2,1)S(1)}, bf16[256,512]{1,0:T(8,128)(2,1)}, u32[]{:S(2)}, u32[]{:S(2)}) collective-permute-start(bf16[256,512]{1,0:T(8,128)(2,1)S(1)} %collective-permute-done.8), channel_id=1, source_target_pairs={{0,30},{2,0},{4,2},{6,4},{8,6},{10,8},{12,10},{14,12},{16,14},{18,... | collective-permute-start | bytes 786440 | tf_op jit(solution)/shard_map/ppermute | solution.py:107
  57.7 8.8 %collective-permute-start.3 = (bf16[256,512]{1,0:T(8,128)(2,1)S(1)}, bf16[256,512]{1,0:T(8,128)(2,1)}, u32[]{:S(2)}, u32[]{:S(2)}) collective-permute-start(bf16[256,512]{1,0:T(8,128)(2,1)S(1)} %collective-permute-done.2), channel_id=1, source_target_pairs={{0,2},{2,4},{4,6},{6,8},{8,10},{10,12},{12,14},{14,16},{16,18},{18... | collective-permute-start | bytes 786440 | tf_op jit(solution)/shard_map/ppermute | solution.py:105
  61.6 9.8 %collective-permute-start.10 = (bf16[256,512]{1,0:T(8,128)(2,1)}, bf16[256,512]{1,0:T(8,128)(2,1)}, u32[]{:S(2)}, u32[]{:S(2)}) collective-permute-start(bf16[256,512]{1,0:T(8,128)(2,1)} %collective-permute-done.9), channel_id=1, source_target_pairs={{0,30},{2,0},{4,2},{6,4},{8,6},{10,8},{12,10},{14,12},{16,14},{18,... | collective-permute-start | bytes 786440 | tf_op jit(solution)/shard_map/ppermute | solution.py:107
  66.5 10.1 %collective-permute-start.4 = (bf16[256,512]{1,0:T(8,128)(2,1)}, bf16[256,512]{1,0:T(8,128)(2,1)}, u32[]{:S(2)}, u32[]{:S(2)}) collective-permute-start(bf16[256,512]{1,0:T(8,128)(2,1)} %collective-permute-done.3), channel_id=1, source_target_pairs={{0,2},{2,4},{4,6},{6,8},{8,10},{10,12},{12,14},{14,16},{16,18},{18... | collective-permute-start | bytes 786440 | tf_op jit(solution)/shard_map/ppermute | solution.py:105
  71.4 56.5 %collective-permute-start.11 = (bf16[256,512]{1,0:T(8,128)(2,1)}, bf16[256,512]{1,0:T(8,128)(2,1)}, u32[]{:S(2)}, u32[]{:S(2)}) collective-permute-start(bf16[256,512]{1,0:T(8,128)(2,1)} %collective-permute-done.10), channel_id=1, source_target_pairs={{0,30},{2,0},{4,2},{6,4},{8,6},{10,8},{12,10},{14,12},{16,14},{18,... | collective-permute-start | bytes 786440 | tf_op jit(solution)/shard_map/ppermute | solution.py:107
  76.6 52.3 %collective-permute-start.5 = (bf16[256,512]{1,0:T(8,128)(2,1)}, bf16[256,512]{1,0:T(8,128)(2,1)}, u32[]{:S(2)}, u32[]{:S(2)}) collective-permute-start(bf16[256,512]{1,0:T(8,128)(2,1)} %collective-permute-done.4), channel_id=1, source_target_pairs={{0,2},{2,4},{4,6},{6,8},{8,10},{10,12},{12,14},{14,16},{16,18},{18... | collective-permute-start | bytes 786440 | tf_op jit(solution)/shard_map/ppermute | solution.py:105
  82.6 46.3 %copy-start.34 = (f32[4,128,128]{2,1,0:T(8,128)S(1)}, f32[4,128,128]{2,1,0:T(8,128)}, u32[]{:S(2)}) copy-start(f32[4,128,128]{2,1,0:T(8,128)} %fusion.96) | copy-start | bytes 786436
  82.6 46.3 %copy-start.36 = (f32[4,8,128]{2,1,0:T(8,128)S(1)}, f32[4,8,128]{2,1,0:T(8,128)}, u32[]{:S(2)}) copy-start(f32[4,8,128]{2,1,0:T(8,128)} %copy-done.35) | copy-start | bytes 49156
  82.7 46.3 %copy-start.38 = (f32[128,4,8]{0,2,1:T(8,128)S(1)}, f32[128,4,8]{0,2,1:T(8,128)}, u32[]{:S(2)}) copy-start(f32[128,4,8]{0,2,1:T(8,128)} %get-tuple-element.991) | copy-start | bytes 49156
  82.7 46.3 %copy-start.45 = (pred[128,128]{1,0:T(8,128)(4,1)S(1)}, pred[128,128]{1,0:T(8,128)(4,1)}, u32[]{:S(2)}) copy-start(pred[128,128]{1,0:T(8,128)(4,1)} %iota_compare_fusion) | copy-start | bytes 49156
  84.0 59.1 %copy-start.6 = (f32[128,2048]{0,1:T(8,128)S(1)}, f32[128,2048]{0,1:T(8,128)}, u32[]{:S(2)}) copy-start(f32[128,2048]{0,1:T(8,128)} %copy-done.5) | copy-start | bytes 3145732
  86.5 42.4 %copy-start.31 = (bf16[128,512]{0,1:T(8,128)(2,1)}, bf16[128,512]{0,1:T(8,128)(2,1)S(1)}, u32[]{:S(2)}) copy-start(bf16[128,512]{0,1:T(8,128)(2,1)S(1)} %copy.166) | copy-start | bytes 393220
  127.9 10.7 %collective-permute-start.12 = (bf16[256,512]{1,0:T(8,128)(2,1)}, bf16[256,512]{1,0:T(8,128)(2,1)S(1)}, u32[]{:S(2)}, u32[]{:S(2)}) collective-permute-start(bf16[256,512]{1,0:T(8,128)(2,1)} %collective-permute-done.11), channel_id=1, source_target_pairs={{0,30},{2,0},{4,2},{6,4},{8,6},{10,8},{12,10},{14,12},{16,14},{18,... | collective-permute-start | bytes 786440 | tf_op jit(solution)/shard_map/ppermute | solution.py:107
  128.9 14.2 %collective-permute-start.6 = (bf16[256,512]{1,0:T(8,128)(2,1)}, bf16[256,512]{1,0:T(8,128)(2,1)S(1)}, u32[]{:S(2)}, u32[]{:S(2)}) collective-permute-start(bf16[256,512]{1,0:T(8,128)(2,1)} %collective-permute-done.5), channel_id=1, source_target_pairs={{0,2},{2,4},{4,6},{6,8},{8,10},{10,12},{12,14},{14,16},{16,18},{18... | collective-permute-start | bytes 786440 | tf_op jit(solution)/shard_map/ppermute | solution.py:105
  138.6 14.0 %collective-permute-start.13 = (bf16[256,512]{1,0:T(8,128)(2,1)S(1)}, bf16[256,512]{1,0:T(8,128)(2,1)S(1)}, u32[]{:S(2)}, u32[]{:S(2)}) collective-permute-start(bf16[256,512]{1,0:T(8,128)(2,1)S(1)} %collective-permute-done.12), channel_id=1, source_target_pairs={{0,30},{2,0},{4,2},{6,4},{8,6},{10,8},{12,10},{14,12},{16,14},{18,... | collective-permute-start | bytes 786440 | tf_op jit(solution)/shard_map/ppermute | solution.py:107
  143.1 14.1 %collective-permute-start.7 = (bf16[256,512]{1,0:T(8,128)(2,1)S(1)}, bf16[256,512]{1,0:T(8,128)(2,1)S(1)}, u32[]{:S(2)}, u32[]{:S(2)}) collective-permute-start(bf16[256,512]{1,0:T(8,128)(2,1)S(1)} %collective-permute-done.6), channel_id=1, source_target_pairs={{0,2},{2,4},{4,6},{6,8},{8,10},{10,12},{12,14},{14,16},{16,18},{18... | collective-permute-start | bytes 786440 | tf_op jit(solution)/shard_map/ppermute | solution.py:105
  152.6 14.1 %collective-permute-start.14 = (bf16[256,512]{1,0:T(8,128)(2,1)S(1)}, bf16[256,512]{1,0:T(8,128)(2,1)S(1)}, u32[]{:S(2)}, u32[]{:S(2)}) collective-permute-start(bf16[256,512]{1,0:T(8,128)(2,1)S(1)} %collective-permute-done.13), channel_id=1, source_target_pairs={{0,30},{2,0},{4,2},{6,4},{8,6},{10,8},{12,10},{14,12},{16,14},{18,... | collective-permute-start | bytes 786440 | tf_op jit(solution)/shard_map/ppermute | solution.py:107
  289.8 183.4 %reduce-scatter.2.cloned.1.call-start = ((), (), s32[]{:S(2)}) async-start(), calls=%async_computation.2 | async-start | bytes 3145728 | tf_op jit(solution)/shard_map/reduce_scatter | solution.py:173
  290.0 54.7 %copy-start.1 = (f32[4,8,64,128]{3,2,1,0:T(8,128)S(1)}, f32[4,8,64,128]{3,2,1,0:T(8,128)}, u32[]{:S(2)}) copy-start(f32[4,8,64,128]{3,2,1,0:T(8,128)} %custom-call.2) | copy-start | bytes 3145732
  290.0 54.7 %copy-start.39 = (f32[4,8]{1,0:T(4,128)S(1)}, f32[4,8]{1,0:T(4,128)}, u32[]{:S(2)}) copy-start(f32[4,8]{1,0:T(4,128)} %custom-call.1) | copy-start | bytes 388
  383.1 56.4 %copy-start.9 = (f32[128,2048]{0,1:T(8,128)S(1)}, f32[128,2048]{0,1:T(8,128)}, u32[]{:S(2)}) copy-start(f32[128,2048]{0,1:T(8,128)} %copy-done.8) | copy-start | bytes 3145732
  383.1 56.4 %copy-start.30 = (bf16[128,512]{0,1:T(8,128)(2,1)S(1)}, bf16[128,512]{0,1:T(8,128)(2,1)}, u32[]{:S(2)}) copy-start(bf16[128,512]{0,1:T(8,128)(2,1)} %copy-done.29) | copy-start | bytes 393220
  383.1 56.4 %copy-start.44 = (f32[128,4,8]{0,2,1:T(8,128)S(1)}, f32[128,4,8]{0,2,1:T(8,128)}, u32[]{:S(2)}) copy-start(f32[128,4,8]{0,2,1:T(8,128)} %get-tuple-element.996) | copy-start | bytes 49156
  (54 other events, 540.3 us)
Sparse Core Ops, SparseCore 0:
  10.2 64.1 all-gather.7
  76.5 138.4 all-gather.9
  217.2 127.4 all-gather.11
  348.0 91.4 all-reduce.1
  442.2 31.0 reduce-scatter.1
